TPU v7x, 128 devices: a whole 4x4x4 slice. The times are simulated.
128 devices in a mesh: rows: 32 (over y, x, core), cols: 4 (over z).
Axes of the slice: x: 4, y: 4, z: 4, core: 2. Of those that a mesh axis runs over, the one named last changes fastest.
Arguments:
- descriptors: bfloat16 [196608, 1024], P('rows'), may hold values from -6 to 6
- struct_atoms: int32 [196608], P('rows'), may hold values from 8 to 512
- env_count: int32 [32], P('rows'), may hold values from 1024 to 6144, as said below
- sparse_desc: bfloat16 [2048, 1024], P('cols'), may hold values from -6 to 6
- panel_pick: int32 [256], replicated, may hold values from 0 to 2047, as said below
Outputs:
- kernel_rows: bfloat16 [196608, 2048], P('rows', 'cols')
- panel_r: float32 [256, 256], P('rows')
- cross_gram: float32 [256, 2048], P('rows', 'cols')
Inputs may be any that keep to these rules, and one draw needn't show every extreme that they name: Row block r holds its environments in its first env_count[r] slots; the rest of its 6144 slots are empty and their contents are ignored. The counts sum to 65536, and in every draw one row block holds exactly 6144. `panel_pick`: the entries are distinct.
All inputs are finite; a program needn't handle non-finite values.
Results may differ from a plain program's by a relative error of at most 0.013.
Values may be sent and summed in bfloat16 or wider, within the bound.
A program may use at most 128 MiB of HBM per device.

v0:
```python
import functools

import jax
import jax.numpy as jnp
from jax import lax
from jax.experimental import pallas as pl
from jax.experimental.pallas import tpu as pltpu
from jax.sharding import PartitionSpec as P

MESH = pl.DeviceIdType.MESH
F32 = jnp.float32
BF16 = jnp.bfloat16
TILE = 8
LANES = 128
MIB = 2**20


def wrap(value, size):
    return jnp.where(value >= size, value - size, value)


def unit_rows(wide):
    mean = jnp.sum(wide * wide, axis=1, keepdims=True) * (1.0 / wide.shape[1])
    return wide * lax.rsqrt(mean + 1e-06)


def each(first, last, body):
    def run(k, carry):
        body(k)
        return carry

    lax.fori_loop(first, last, run, 0)


def gram_kernel(
    n_rows, n_cols, env_total, block,
    pick_ref, count_ref, atoms_ref, sparse_ref, x_ref,
    rows_ref, whole_ref, sum_ref,
    xbuf, kbuf, factor, units, gathered, zbuf, gram, gbuf, total_gram, cross, cbuf,
    picks, count, xsem, osem, isem, zsend, zrecv, psend, fsend, precv, gsend, csend, wsend, rsem,
):
    me = lax.axis_index("rows")
    group = lax.axis_index("cols")
    chip, core = me // 2, lax.rem(me, 2)
    n_chips = n_rows // 2
    slots, depth = xbuf.shape
    width, panel = units.shape[0], gathered.shape[0]
    half, short = depth // 2, width // 2

    def rows_of(i, size):
        return pl.ds(pl.multiple_of(i * size, size), size)

    load_units = pltpu.make_async_copy(sparse_ref, units, isem.at[0])
    load_picks = pltpu.make_async_copy(pick_ref, picks, isem.at[1])
    load_count = pltpu.make_async_copy(count_ref, count, isem.at[2])
    load_units.start()
    load_picks.start()
    load_count.start()
    loads = [
        pltpu.make_async_copy(
            x_ref.at[pl.ds(i * block, block), :], xbuf.at[pl.ds(i * block, block), :], xsem.at[i]
        )
        for i in range(slots // block)
    ]
    for copy in loads:
        copy.start()

    barrier = pltpu.get_barrier_semaphore()
    each(1, n_rows, lambda k: pl.semaphore_signal(
        barrier, inc=1, device_id=(wrap(me + k, n_rows), group), device_id_type=MESH))
    for k in range(1, n_cols):
        pl.semaphore_signal(
            barrier, inc=1, device_id=(me, wrap(group + k, n_cols)), device_id_type=MESH
        )

    load_units.wait()

    load_picks.wait()
    column = lax.broadcasted_iota(jnp.int32, (16, width), 1) + group * width
    row = lax.broadcasted_iota(jnp.int32, (16, width), 0)
    wanted = jnp.zeros((16, width), jnp.int32)
    for i in range(16):
        wanted = jnp.where(row == i, picks[chip * 16 + i], wanted)
    one_hot = jnp.where(wanted == column, 1.0, 0.0).astype(BF16)
    chosen = unit_rows(jnp.dot(one_hot, units[...], preferred_element_type=F32))
    zbuf[group] = jnp.where(core == 0, chosen[:, :half], chosen[:, half:]).astype(BF16)

    def z_copy(k):
        return pltpu.make_async_remote_copy(
            src_ref=zbuf.at[group], dst_ref=zbuf.at[group],
            send_sem=zsend.at[k - 1], recv_sem=zrecv.at[k - 1],
            device_id=(me, wrap(group + k, n_cols)), device_id_type=MESH,
        )

    pl.semaphore_wait(barrier, n_rows - 1 + n_cols - 1)
    for k in range(1, n_cols):
        z_copy(k).start()

    def normalise(i):
        at = rows_of(i, 64)
        units[at, :] = unit_rows(units[at, :].astype(F32)).astype(BF16)

    each(0, width // 64, normalise)
    load_count.wait()
    lines = atoms_ref.shape[0]
    weight = (8.0 * lax.rsqrt(atoms_ref[...].astype(F32))).astype(BF16).astype(F32)
    slot = (
        lax.broadcasted_iota(jnp.int32, atoms_ref.shape, 0) * LANES
        + lax.broadcasted_iota(jnp.int32, atoms_ref.shape, 1)
    )
    columns = jnp.where(slot < count[0], jnp.sqrt(weight * (1.0 / depth)), 0.0).T
    for i in range(lines):
        factor[i * LANES : (i + 1) * LANES, :] = columns[:, i : i + 1]

    def save(i):
        return pltpu.make_async_copy(
            kbuf.at[pl.ds(i * block, block), pl.ds(0, width)],
            rows_ref.at[pl.ds(i * block, block), :],
            osem.at[i],
        )

    def own_points(i):
        at = slice(i * block, (i + 1) * block)
        loads[i].wait()
        x = xbuf[at, :]
        wide = x.astype(F32)
        mean = jnp.sum(wide * wide, axis=1, keepdims=True) * (1.0 / depth)
        scale = factor[at, :] * lax.rsqrt(mean + 1e-06)
        factor[at, :] = scale
        inner = lax.dot_general(
            x, units[...], (((1,), (1,)), ((), ())), preferred_element_type=F32
        ) * scale
        kbuf[at, :width] = (inner * inner).astype(BF16)
        save(i).start()

    def panel_points(i):
        at = slice(i * block, (i + 1) * block)
        inner = lax.dot_general(
            xbuf[at, :], gathered[...], (((1,), (1,)), ((), ())), preferred_element_type=F32
        ) * factor[at, :]
        kbuf[at, width:] = (inner * inner).astype(BF16)

    own_points(0)

    for k in range(1, n_cols):
        z_copy(k).wait()
    total = zbuf[0].astype(F32)
    for k in range(1, n_cols):
        total = total + zbuf[k].astype(F32)

    def piece(which_chip, which_core):
        return gathered.at[rows_of(which_chip, 16), rows_of(which_core, half)]

    piece(chip, core)[...] = total.astype(BF16)

    def plane_copy(k):
        return pltpu.make_async_remote_copy(
            src_ref=piece(chip, core), dst_ref=piece(chip, core),
            send_sem=psend.at[k], recv_sem=precv.at[core, chip],
            device_id=(wrap(chip + k, n_chips) * 2 + core, group), device_id_type=MESH,
        )

    def core_copy(source):
        return pltpu.make_async_remote_copy(
            src_ref=piece(source, core), dst_ref=piece(source, core),
            send_sem=fsend.at[source], recv_sem=precv.at[core, source],
            device_id=(chip * 2 + 1 - core, group), device_id_type=MESH,
        )

    def arrival(source, which_core):
        return pltpu.make_async_copy(
            piece(source, which_core), piece(source, which_core), precv.at[which_core, source]
        )

    each(1, n_chips, lambda k: plane_copy(k).start())
    core_copy(chip).start()
    for i in range(1, slots // block):
        own_points(i)

    def forward(k):
        source = wrap(chip + n_chips - k, n_chips)
        arrival(source, core).wait()
        core_copy(source).start()

    each(1, n_chips, forward)

    def finish(k):
        source = wrap(chip + n_chips - k, n_chips)
        arrival(source, 1 - core).wait()

    each(0, n_chips, finish)
    for i in range(slots // block):
        panel_points(i)

    def transposed_product(right):
        return lax.dot_general(
            kbuf[:, width:], right, (((0,), (0,)), ((), ())), preferred_element_type=F32
        ) * (1.0 / env_total)

    gram[...] = transposed_product(kbuf[:, width:])

    def gram_copy(k):
        peer = wrap(me + k, n_rows)
        return pltpu.make_async_remote_copy(
            src_ref=gram.at[rows_of(peer, TILE), :], dst_ref=gbuf.at[k - 1],
            send_sem=gsend.at[k], recv_sem=rsem.at[0],
            device_id=(peer, group), device_id_type=MESH,
        )

    def cross_copy(k):
        peer = wrap(me + k, n_rows)
        return pltpu.make_async_remote_copy(
            src_ref=cross.at[peer], dst_ref=cbuf.at[k - 1],
            send_sem=csend.at[k], recv_sem=rsem.at[1],
            device_id=(peer, group), device_id_type=MESH,
        )

    def whole_copy(k):
        return pltpu.make_async_remote_copy(
            src_ref=total_gram.at[rows_of(me, TILE), :],
            dst_ref=total_gram.at[rows_of(me, TILE), :],
            send_sem=wsend.at[k], recv_sem=rsem.at[2],
            device_id=(wrap(me + k, n_rows), group), device_id_type=MESH,
        )

    each(1, n_rows, lambda k: gram_copy(k).start())
    product = transposed_product(kbuf[:, :width])
    for r in range(panel // TILE):
        part = product[r * TILE : (r + 1) * TILE, :]
        cross[r] = jnp.concatenate([part[:, :short], part[:, short:]], axis=0).astype(BF16)
    each(1, n_rows, lambda k: cross_copy(k).start())
    pltpu.make_async_copy(gbuf, gbuf, rsem.at[0]).wait()
    total = gram[rows_of(me, TILE), :]
    for r in range(n_rows - 1):
        total = total + gbuf[r]
    total_gram[rows_of(me, TILE), :] = total
    each(1, n_rows, lambda k: whole_copy(k).start())
    pltpu.make_async_copy(cbuf, cbuf, rsem.at[1]).wait()
    total = cross[me].astype(F32)
    for r in range(n_rows - 1):
        total = total + cbuf[r].astype(F32)
    sum_ref[:, :short] = total[:TILE]
    sum_ref[:, short:] = total[TILE:]
    arrived = total_gram.at[pl.ds(0, panel - TILE), :]
    pltpu.make_async_copy(arrived, arrived, rsem.at[2]).wait()
    whole_ref[...] = total_gram[...]

    def all_sent(k):
        gram_copy(k).wait_send()
        cross_copy(k).wait_send()
        whole_copy(k).wait_send()

    each(1, n_rows, all_sent)
    each(1, n_chips, lambda k: plane_copy(k).wait_send())
    each(0, n_chips, lambda k: core_copy(k).wait_send())
    for i in range(slots // block):
        save(i).wait()


def gram_pass(panel_pick, env_count, struct_atoms, sparse_desc, descriptors, n_rows, n_cols, block):
    slots, depth = descriptors.shape
    width, panel = sparse_desc.shape[0], panel_pick.shape[0]
    n_chips = n_rows // 2
    short = width // 2
    hbm = pl.BlockSpec(memory_space=pl.ANY)
    vmem = pl.BlockSpec(memory_space=pltpu.VMEM)
    dma = pltpu.SemaphoreType.DMA
    return pl.pallas_call(
        functools.partial(gram_kernel, n_rows, n_cols, slots // 3 * n_rows, block),
        out_shape=(
            jax.ShapeDtypeStruct((slots, width), BF16),
            jax.ShapeDtypeStruct((panel, panel), F32),
            jax.ShapeDtypeStruct((TILE, width), F32),
        ),
        in_specs=[hbm, hbm, vmem, hbm, hbm],
        out_specs=(hbm, vmem, vmem),
        scratch_shapes=[
            pltpu.VMEM((slots, depth), BF16),
            pltpu.VMEM((slots, width + panel), BF16),
            pltpu.VMEM((slots, 1), F32),
            pltpu.VMEM((width, depth), BF16),
            pltpu.VMEM((panel, depth), BF16),
            pltpu.VMEM((n_cols, 16, depth // 2), BF16),
            pltpu.VMEM((panel, panel), F32),
            pltpu.VMEM((n_rows - 1, TILE, panel), F32),
            pltpu.VMEM((panel, panel), F32),
            pltpu.VMEM((n_rows, 2 * TILE, short), BF16),
            pltpu.VMEM((n_rows - 1, 2 * TILE, short), BF16),
            pltpu.SMEM((panel,), jnp.int32),
            pltpu.SMEM((1,), jnp.int32),
            dma((slots // block,)),
            dma((slots // block,)),
            dma((3,)),
            dma((n_cols - 1,)),
            dma((n_cols - 1,)),
            dma((n_chips,)),
            dma((n_chips,)),
            dma((2, n_chips)),
            dma((n_rows,)),
            dma((n_rows,)),
            dma((n_rows,)),
            dma((3,)),
        ],
        compiler_params=pltpu.CompilerParams(
            collective_id=0, has_side_effects=True, vmem_limit_bytes=56 * MIB
        ),
        name="gram_pass",
    )(panel_pick, env_count, struct_atoms.reshape(slots // LANES, LANES), sparse_desc, descriptors)


def wide_of(tile, lane):
    return jnp.broadcast_to(tile[:, lane : lane + 1], (TILE, LANES))


def tall_of(tile, line):
    return jnp.broadcast_to(tile[line : line + 1, :], (TILE, LANES))


def factor_band(tiles):
    groups, halves = len(tiles), len(tiles[0])
    line = lax.broadcasted_iota(jnp.int32, (TILE, LANES), 0)
    out = []
    for t in range(groups):
        base = t * TILE
        cols = {g: [wide_of(tiles[g][0], base + k) for k in range(TILE)] for g in range(t, groups)}
        low = {(i, k): tall_of(cols[t][k], i) for k in range(TILE) for i in range(k, TILE)}
        inv = []
        for k in range(TILE):
            inv.append(lax.rsqrt(low[k, k]))
            for i in range(k + 1, TILE):
                low[i, k] = low[i, k] * inv[k]
            for m in range(k + 1, TILE):
                for i in range(m, TILE):
                    low[i, m] = low[i, m] - low[i, k] * low[m, k]
        band = []
        for h in range(halves):
            lines = []
            for k in range(TILE):
                value = tall_of(tiles[t][h], k)
                for m in range(k):
                    value = value - low[k, m] * lines[m]
                lines.append(value * inv[k])
            band.append(lines)
        merged = []
        for h in range(halves):
            value = band[h][0]
            for k in range(1, TILE):
                value = jnp.where(line == k, band[h][k], value)
            merged.append(value)
        out.append(merged)
        for g in range(t + 1, groups):
            left = []
            for k in range(TILE):
                value = cols[g][k]
                for m in range(k):
                    value = value - left[m] * low[k, m]
                left.append(value * inv[k])
            for h in range(halves):
                value = tiles[g][h]
                for k in range(TILE):
                    value = value - left[k] * band[h][k]
                tiles[g][h] = value
    return out


def factor_kernel(
    gram_ref, rows_ref, sum_ref, out_ref, kernel_ref, cross_ref, work, passing, sums, isem, osem
):
    size = gram_ref.shape[0]
    parts = osem.shape[0] - 1
    part = rows_ref.shape[0] // parts
    chunks = [pl.ds(i * part, part) for i in range(parts)]
    load = pltpu.make_async_copy(gram_ref, work, isem.at[parts])
    loads = [
        pltpu.make_async_copy(rows_ref.at[c, :], passing.at[c, :], isem.at[i])
        for i, c in enumerate(chunks)
    ]
    loads.append(pltpu.make_async_copy(sum_ref, sums, isem.at[parts + 1]))
    saves = [
        pltpu.make_async_copy(passing.at[c, :], kernel_ref.at[c, :], osem.at[i])
        for i, c in enumerate(chunks)
    ]
    saves.append(pltpu.make_async_copy(sums, cross_ref, osem.at[parts]))
    load.start()
    for copy in loads:
        copy.start()
    load.wait()
    bands = size // LANES
    groups = LANES // TILE
    line = lax.broadcasted_iota(jnp.int32, (TILE, LANES), 0)
    lane = lax.broadcasted_iota(jnp.int32, (TILE, LANES), 1)
    for b in range(bands):
        tiles = [
            [
                work[b * LANES + g * TILE : b * LANES + (g + 1) * TILE, h * LANES : (h + 1) * LANES]
                for h in range(b, bands)
            ]
            for g in range(groups)
        ]
        factor = factor_band(tiles)
        for g in range(groups):
            first = b * LANES + g * TILE
            for h in range(bands):
                if h < b:
                    value = jnp.zeros((TILE, LANES), F32)
                else:
                    value = factor[g][h - b]
                    if h == b:
                        value = jnp.where(lane >= line + g * TILE, value, 0.0)
                work[first : first + TILE, h * LANES : (h + 1) * LANES] = value
        if b == 0:
            for copy, then in zip(loads, saves, strict=True):
                copy.wait()
                then.start()
        if b + 1 < bands:
            right = work[b * LANES : (b + 1) * LANES, (b + 1) * LANES :]
            work[(b + 1) * LANES :, (b + 1) * LANES :] -= lax.dot_general(
                right, right, (((0,), (0,)), ((), ())),
                precision=lax.Precision.HIGHEST, preferred_element_type=F32,
            )
    me = lax.axis_index("rows")
    out_ref[...] = work[pl.ds(pl.multiple_of(me * TILE, TILE), TILE), :]
    for copy in saves:
        copy.wait()


def factor_pass(gram, kernel_rows, cross_sum):
    size = gram.shape[0]
    hbm = pl.BlockSpec(memory_space=pl.ANY)
    vmem = pl.BlockSpec(memory_space=pltpu.VMEM)
    return pl.pallas_call(
        factor_kernel,
        out_shape=(
            jax.ShapeDtypeStruct((TILE, size), F32),
            jax.ShapeDtypeStruct(kernel_rows.shape, BF16),
            jax.ShapeDtypeStruct(cross_sum.shape, F32),
        ),
        in_specs=[hbm, hbm, hbm],
        out_specs=(vmem, hbm, hbm),
        scratch_shapes=[
            pltpu.VMEM((size, size), F32),
            pltpu.VMEM(kernel_rows.shape, BF16),
            pltpu.VMEM(cross_sum.shape, F32),
            pltpu.SemaphoreType.DMA((8,)),
            pltpu.SemaphoreType.DMA((7,)),
        ],
        compiler_params=pltpu.CompilerParams(vmem_limit_bytes=60 * MIB),
        name="factor_pass",
    )(gram, kernel_rows, cross_sum)


def local(descriptors, struct_atoms, env_count, sparse_desc, panel_pick):
    n_rows, n_cols = lax.axis_size("rows"), lax.axis_size("cols")
    kernel_rows, gram, cross_sum = gram_pass(
        panel_pick, env_count, struct_atoms, sparse_desc, descriptors, n_rows, n_cols, 2048
    )
    factor_rows, kernel_rows, cross_gram = factor_pass(gram, kernel_rows, cross_sum)
    return kernel_rows, factor_rows, cross_gram


def solution(mesh):
    return jax.shard_map(
        local,
        mesh=mesh,
        in_specs=(P("rows", None), P("rows"), P("rows"), P("cols", None), P()),
        out_specs=(P("rows", "cols"), P("rows", None), P("rows", "cols")),
        check_vma=False,
    )
```

profile of v0, /device:TPU:1, one launch (start us, length us, event | category | flops | bytes accessed | tf_op | source)
XLA Modules:
  0.0 53.2 jit_solution(11839031172586187315)
XLA Ops:
  1.3 41.0 %gram_pass.1 = (bf16[6144,512]{1,0:T(8,128)(2,1)}, f32[256,256]{1,0:T(8,128)}, f32[8,512]{1,0:T(8,128)}) custom-call(s32[256]{0:T(256)} %pick_ref.1, s32[1]{0:T(128)S(6)} %copy.8.count_ref, s32[48,128]{1,0:T(8,128)} %bitcast.1, bf16[512,1024]{1,0:T(8,128)(2,1)} %sparse_ref.1, bf16[6144,1024]{1,0:T(8,128)(2,1)} %x_ref.1), custom_call_target="tpu_custom_call" | custom-call | tf_op jit(solution)/shard_map/gram_pass/pallas_call | solution.py:268
  42.3 10.7 %factor_pass.1 = (f32[8,256]{1,0:T(8,128)}, bf16[6144,512]{1,0:T(8,128)(2,1)}, f32[8,512]{1,0:T(8,128)}) custom-call(f32[256,256]{1,0:T(8,128)} %get-tuple-element.9.gram_ref, bf16[6144,512]{1,0:T(8,128)(2,1)} %get-tuple-element.10.rows_ref, f32[8,512]{1,0:T(8,128)} %get-tuple-element.11.sum_ref), custom_call_target="tpu_custom_call" | custom-call | tf_op jit(solution)/shard_map/factor_pass/pallas_call | solution.py:431
where the time goes:
time: 53.4 us; the launch traced here: 53.2 us
  Pallas kernels  51.7 us (97%)
  between operations  1.47 us (3%)
    pallas_call x1, Pallas kernels, gram_pass(): pl.pallas_call(functools.partial(gram_kernel, n_rows, n_cols, slots // 3...  41 us
    pallas_call x1, Pallas kernels, factor_pass(): pl.pallas_call(factor_kernel, out_shape=(jax.ShapeDtypeStruct((TILE, size...  10.7 us

commit v1 on v0

--- a/solution.py
+++ b/solution.py
@@ -12,6 +12,7 @@
 BF16 = jnp.bfloat16
 TILE = 8
 LANES = 128
+BAND = 64
 MIB = 2**20
 
 
@@ -36,7 +37,7 @@
     n_rows, n_cols, env_total, block,
     pick_ref, count_ref, atoms_ref, sparse_ref, x_ref,
     rows_ref, whole_ref, sum_ref,
-    xbuf, kbuf, factor, units, gathered, zbuf, gram, gbuf, total_gram, cross, cbuf,
+    xbuf, kbuf, partial, factor, columns, units, gathered, zbuf, gram, gbuf, total_gram, cross, cbuf,
     picks, count, xsem, osem, isem, zsend, zrecv, psend, fsend, precv, gsend, csend, wsend, rsem,
 ):
     me = lax.axis_index("rows")
@@ -56,14 +57,11 @@
     load_units.start()
     load_picks.start()
     load_count.start()
-    loads = [
-        pltpu.make_async_copy(
-            x_ref.at[pl.ds(i * block, block), :], xbuf.at[pl.ds(i * block, block), :], xsem.at[i]
-        )
-        for i in range(slots // block)
-    ]
-    for copy in loads:
-        copy.start()
+    def load(i):
+        at = rows_of(i, block)
+        return pltpu.make_async_copy(x_ref.at[at, :], xbuf.at[at, :], xsem.at[i])
+
+    each(0, slots // block, lambda i: load(i).start())
 
     barrier = pltpu.get_barrier_semaphore()
     each(1, n_rows, lambda k: pl.semaphore_signal(
@@ -96,51 +94,65 @@
     for k in range(1, n_cols):
         z_copy(k).start()
 
-    def normalise(i):
-        at = rows_of(i, 64)
-        units[at, :] = unit_rows(units[at, :].astype(F32)).astype(BF16)
-
-    each(0, width // 64, normalise)
+    for i in range(0, width, 128):
+        units[i : i + 128, :] = unit_rows(units[i : i + 128, :].astype(F32)).astype(BF16)
     load_count.wait()
-    lines = atoms_ref.shape[0]
     weight = (8.0 * lax.rsqrt(atoms_ref[...].astype(F32))).astype(BF16).astype(F32)
     slot = (
         lax.broadcasted_iota(jnp.int32, atoms_ref.shape, 0) * LANES
         + lax.broadcasted_iota(jnp.int32, atoms_ref.shape, 1)
     )
-    columns = jnp.where(slot < count[0], jnp.sqrt(weight * (1.0 / depth)), 0.0).T
-    for i in range(lines):
-        factor[i * LANES : (i + 1) * LANES, :] = columns[:, i : i + 1]
+    roots = jnp.where(slot < count[0], jnp.sqrt(weight * (1.0 / depth)), 0.0).T
+    lines = block // LANES
+    blocks = slots // block
+    for i in range(blocks):
+        columns[i] = roots[:, i * lines : (i + 1) * lines]
 
     def save(i):
+        at = rows_of(i, block)
         return pltpu.make_async_copy(
-            kbuf.at[pl.ds(i * block, block), pl.ds(0, width)],
-            rows_ref.at[pl.ds(i * block, block), :],
-            osem.at[i],
-        )
-
-    def own_points(i):
-        at = slice(i * block, (i + 1) * block)
-        loads[i].wait()
-        x = xbuf[at, :]
-        wide = x.astype(F32)
+            kbuf.at[at, pl.ds(0, width)], rows_ref.at[at, :], osem.at[i]
+        )
+
+    def norms(first, last):
+        each(first, last, lambda i: load(i).wait())
+        at = slice(first * block, last * block)
+        wide = xbuf[at, :].astype(F32)
         mean = jnp.sum(wide * wide, axis=1, keepdims=True) * (1.0 / depth)
-        scale = factor[at, :] * lax.rsqrt(mean + 1e-06)
-        factor[at, :] = scale
+        root = jnp.concatenate(
+            [columns[i][:, j : j + 1] for i in range(first, last) for j in range(lines)], axis=0
+        )
+        factor[at, :] = jnp.broadcast_to(
+            root * lax.rsqrt(mean + 1e-06), ((last - first) * block, LANES)
+        )
+
+    def kernel_of(at, points):
         inner = lax.dot_general(
-            x, units[...], (((1,), (1,)), ((), ())), preferred_element_type=F32
-        ) * scale
-        kbuf[at, :width] = (inner * inner).astype(BF16)
-        save(i).start()
-
-    def panel_points(i):
-        at = slice(i * block, (i + 1) * block)
-        inner = lax.dot_general(
-            xbuf[at, :], gathered[...], (((1,), (1,)), ((), ())), preferred_element_type=F32
-        ) * factor[at, :]
+            xbuf[at, :], points[...], (((1,), (1,)), ((), ())), preferred_element_type=F32
+        ) * jnp.concatenate([factor[at, :]] * (points.shape[0] // LANES), axis=1)
+        return (inner * inner).astype(BF16)
+
+    def own_points(first, last):
+        at = slice(first * block, last * block)
+        kbuf[at, :width] = kernel_of(at, units)
+        each(first, last, lambda i: save(i).start())
+
+    def panel_half(at, which):
+        across = rows_of(which, half)
+        return lax.dot_general(
+            xbuf[at, across], gathered[:, across], (((1,), (1,)), ((), ())),
+            preferred_element_type=F32,
+        )
+
+    def panel_points(at):
+        inner = partial[at, :] + panel_half(at, 1 - core)
+        inner = inner * jnp.concatenate([factor[at, :]] * (panel // LANES), axis=1)
         kbuf[at, width:] = (inner * inner).astype(BF16)
 
-    own_points(0)
+    third = blocks // 3
+    late = 2 * third
+    norms(0, third)
+    own_points(0, third)
 
     for k in range(1, n_cols):
         z_copy(k).wait()
@@ -174,8 +186,10 @@
 
     each(1, n_chips, lambda k: plane_copy(k).start())
     core_copy(chip).start()
-    for i in range(1, slots // block):
-        own_points(i)
+    norms(third, late)
+    own_points(third, late)
+    norms(late, blocks)
+    own_points(late, blocks)
 
     def forward(k):
         source = wrap(chip + n_chips - k, n_chips)
@@ -184,13 +198,17 @@
 
     each(1, n_chips, forward)
 
+    parts = [slice(i * slots // 3, (i + 1) * slots // 3) for i in range(3)]
+    for at in parts:
+        partial[at, :] = panel_half(at, core)
+
     def finish(k):
         source = wrap(chip + n_chips - k, n_chips)
         arrival(source, 1 - core).wait()
 
     each(0, n_chips, finish)
-    for i in range(slots // block):
-        panel_points(i)
+    for at in parts:
+        panel_points(at)
 
     def transposed_product(right):
         return lax.dot_general(
@@ -253,8 +271,7 @@
     each(1, n_rows, all_sent)
     each(1, n_chips, lambda k: plane_copy(k).wait_send())
     each(0, n_chips, lambda k: core_copy(k).wait_send())
-    for i in range(slots // block):
-        save(i).wait()
+    each(0, blocks, lambda i: save(i).wait())
 
 
 def gram_pass(panel_pick, env_count, struct_atoms, sparse_desc, descriptors, n_rows, n_cols, block):
@@ -277,7 +294,9 @@
         scratch_shapes=[
             pltpu.VMEM((slots, depth), BF16),
             pltpu.VMEM((slots, width + panel), BF16),
-            pltpu.VMEM((slots, 1), F32),
+            pltpu.VMEM((slots, panel), F32),
+            pltpu.VMEM((slots, LANES), F32),
+            pltpu.VMEM((slots // block, LANES, block // LANES), F32),
             pltpu.VMEM((width, depth), BF16),
             pltpu.VMEM((panel, depth), BF16),
             pltpu.VMEM((n_cols, 16, depth // 2), BF16),
@@ -316,22 +335,27 @@
     return jnp.broadcast_to(tile[line : line + 1, :], (TILE, LANES))
 
 
-def factor_band(tiles):
+def factor_band(tiles, first):
     groups, halves = len(tiles), len(tiles[0])
     line = lax.broadcasted_iota(jnp.int32, (TILE, LANES), 0)
     out = []
     for t in range(groups):
-        base = t * TILE
+        base = first + t * TILE
         cols = {g: [wide_of(tiles[g][0], base + k) for k in range(TILE)] for g in range(t, groups)}
         low = {(i, k): tall_of(cols[t][k], i) for k in range(TILE) for i in range(k, TILE)}
         inv = []
-        for k in range(TILE):
-            inv.append(lax.rsqrt(low[k, k]))
+        for k in range(0, TILE, 2):
+            top, mixed, bottom = low[k, k], low[k + 1, k], low[k + 1, k + 1]
+            root = lax.rsqrt(top)
+            inv.append(root)
+            inv.append(top * root * lax.rsqrt(top * bottom - mixed * mixed))
             for i in range(k + 1, TILE):
-                low[i, k] = low[i, k] * inv[k]
-            for m in range(k + 1, TILE):
+                low[i, k] = low[i, k] * root
+            for i in range(k + 2, TILE):
+                low[i, k + 1] = (low[i, k + 1] - low[i, k] * low[k + 1, k]) * inv[k + 1]
+            for m in range(k + 2, TILE):
                 for i in range(m, TILE):
-                    low[i, m] = low[i, m] - low[i, k] * low[m, k]
+                    low[i, m] = low[i, m] - (low[i, k] * low[m, k] + low[i, k + 1] * low[m, k + 1])
         band = []
         for h in range(halves):
             lines = []
@@ -356,10 +380,10 @@
                     value = value - left[m] * low[k, m]
                 left.append(value * inv[k])
             for h in range(halves):
-                value = tiles[g][h]
-                for k in range(TILE):
-                    value = value - left[k] * band[h][k]
-                tiles[g][h] = value
+                terms = [left[k] * band[h][k] for k in range(TILE)]
+                while len(terms) > 1:
+                    terms = [x + y for x, y in zip(terms[::2], terms[1::2], strict=True)]
+                tiles[g][h] = tiles[g][h] - terms[0]
     return out
 
 
@@ -385,41 +409,55 @@
     for copy in loads:
         copy.start()
     load.wait()
-    bands = size // LANES
-    groups = LANES // TILE
+    halves = size // LANES
     line = lax.broadcasted_iota(jnp.int32, (TILE, LANES), 0)
     lane = lax.broadcasted_iota(jnp.int32, (TILE, LANES), 1)
-    for b in range(bands):
+
+    def tile(g, h):
+        return slice(g * TILE, (g + 1) * TILE), slice(h * LANES, (h + 1) * LANES)
+
+    tall, wide, diagonal = [], [], []
+    for h in range(halves):
+        along = jnp.zeros((TILE, LANES), F32)
+        for g in range(h * LANES // TILE, (h + 1) * LANES // TILE):
+            there = jnp.where(lane == line + (g * TILE - h * LANES), work[tile(g, h)], 0.0)
+            tall.append(lax.rsqrt(jnp.sum(there, axis=1, keepdims=True)))
+            along = along + there
+        diagonal.append(jnp.sum(along, axis=0, keepdims=True))
+        wide.append(lax.rsqrt(diagonal[h]))
+    for g in range(size // TILE):
+        for h in range(g * TILE // LANES, halves):
+            work[tile(g, h)] = work[tile(g, h)] * tall[g] * wide[h]
+    for start in range(0, size, BAND):
+        end, near = start + BAND, start // LANES
         tiles = [
-            [
-                work[b * LANES + g * TILE : b * LANES + (g + 1) * TILE, h * LANES : (h + 1) * LANES]
-                for h in range(b, bands)
-            ]
-            for g in range(groups)
+            [work[tile(g, h)] for h in range(near, halves)]
+            for g in range(start // TILE, end // TILE)
         ]
-        factor = factor_band(tiles)
-        for g in range(groups):
-            first = b * LANES + g * TILE
-            for h in range(bands):
-                if h < b:
-                    value = jnp.zeros((TILE, LANES), F32)
-                else:
-                    value = factor[g][h - b]
-                    if h == b:
-                        value = jnp.where(lane >= line + g * TILE, value, 0.0)
-                work[first : first + TILE, h * LANES : (h + 1) * LANES] = value
-        if b == 0:
+        factor = factor_band(tiles, start % LANES)
+        for i, parts_of in enumerate(factor):
+            g = start // TILE + i
+            for h in range(halves):
+                value = jnp.zeros((TILE, LANES), F32) if h < near else parts_of[h - near]
+                if h == near:
+                    value = jnp.where(lane >= line + (g * TILE - h * LANES), value, 0.0)
+                work[tile(g, h)] = value
+        if start == 0:
             for copy, then in zip(loads, saves, strict=True):
                 copy.wait()
                 then.start()
-        if b + 1 < bands:
-            right = work[b * LANES : (b + 1) * LANES, (b + 1) * LANES :]
-            work[(b + 1) * LANES :, (b + 1) * LANES :] -= lax.dot_general(
+        if end < size:
+            far = end // LANES * LANES
+            right = work[start:end, far:]
+            inner = lax.dot_general(
                 right, right, (((0,), (0,)), ((), ())),
                 precision=lax.Precision.HIGHEST, preferred_element_type=F32,
             )
+            work[end:, far:] -= inner[end - far :, :]
     me = lax.axis_index("rows")
-    out_ref[...] = work[pl.ds(pl.multiple_of(me * TILE, TILE), TILE), :]
+    out_ref[...] = work[pl.ds(pl.multiple_of(me * TILE, TILE), TILE), :] * jnp.concatenate(
+        [diagonal[h] * wide[h] for h in range(halves)], axis=1
+    )
     for copy in saves:
         copy.wait()
 
@@ -452,7 +490,7 @@
 def local(descriptors, struct_atoms, env_count, sparse_desc, panel_pick):
     n_rows, n_cols = lax.axis_size("rows"), lax.axis_size("cols")
     kernel_rows, gram, cross_sum = gram_pass(
-        panel_pick, env_count, struct_atoms, sparse_desc, descriptors, n_rows, n_cols, 2048
+        panel_pick, env_count, struct_atoms, sparse_desc, descriptors, n_rows, n_cols, 512
     )
     factor_rows, kernel_rows, cross_gram = factor_pass(gram, kernel_rows, cross_sum)
     return kernel_rows, factor_rows, cross_gram

time: 53.4 us -> 52.2 us (0.978)
  Pallas kernels: 51.7 us -> 50.5 us
    pallas_call x1, Pallas kernels: 10.7 us -> 9.54 us  [factor_pass(): pl.pallas_call(factor_kernel, out_shape=(jax.ShapeDtypeStruct((TILE, size...]
where the time goes in v1:
time: 52.2 us; the launch traced here: 52 us
  Pallas kernels  50.5 us (97%)
  between operations  1.45 us (3%)
    pallas_call x1, Pallas kernels, gram_pass(): pl.pallas_call(functools.partial(gram_kernel, n_rows, n_cols, slots // 3...  41 us
    pallas_call x1, Pallas kernels, factor_pass(): pl.pallas_call(factor_kernel, out_shape=(jax.ShapeDtypeStruct((TILE, size...  9.54 us

profile of v1, /device:TPU:1, one launch (start us, length us, event | category | flops | bytes accessed | tf_op | source)
XLA Modules:
  0.0 52.0 jit_solution(8118979652318973402)
XLA Ops:
  1.3 41.0 %gram_pass.1 = (bf16[6144,512]{1,0:T(8,128)(2,1)}, f32[256,256]{1,0:T(8,128)}, f32[8,512]{1,0:T(8,128)}) custom-call(s32[256]{0:T(256)} %pick_ref.1, s32[1]{0:T(128)S(6)} %copy.8.count_ref, s32[48,128]{1,0:T(8,128)} %bitcast.1, bf16[512,1024]{1,0:T(8,128)(2,1)} %sparse_ref.1, bf16[6144,1024]{1,0:T(8,128)(2,1)} %x_ref.1), custom_call_target="tpu_custom_call" | custom-call | tf_op jit(solution)/shard_map/gram_pass/pallas_call | solution.py:285
  42.3 9.5 %factor_pass.1 = (f32[8,256]{1,0:T(8,128)}, bf16[6144,512]{1,0:T(8,128)(2,1)}, f32[8,512]{1,0:T(8,128)}) custom-call(f32[256,256]{1,0:T(8,128)} %get-tuple-element.9.gram_ref, bf16[6144,512]{1,0:T(8,128)(2,1)} %get-tuple-element.10.rows_ref, f32[8,512]{1,0:T(8,128)} %get-tuple-element.11.sum_ref), custom_call_target="tpu_custom_call" | custom-call | tf_op jit(solution)/shard_map/factor_pass/pallas_call | solution.py:469

commit v2 on v1

--- a/solution.py
+++ b/solution.py
@@ -37,8 +37,8 @@
     n_rows, n_cols, env_total, block,
     pick_ref, count_ref, atoms_ref, sparse_ref, x_ref,
     rows_ref, whole_ref, sum_ref,
-    xbuf, kbuf, partial, factor, columns, units, gathered, zbuf, gram, gbuf, total_gram, cross, cbuf,
-    picks, count, xsem, osem, isem, zsend, zrecv, psend, fsend, precv, gsend, csend, wsend, rsem,
+    xbuf, kbuf, partial, factor, columns, units, gathered, zbuf, gram, gbuf, lbuf, total_gram, cross, cbuf, sumbuf,
+    picks, count, xsem, osem, isem, zsend, zrecv, psend, fsend, precv, gsend, csend, wsend, lsend, vsend, rsem,
 ):
     me = lax.axis_index("rows")
     group = lax.axis_index("cols")
@@ -217,12 +217,22 @@
 
     gram[...] = transposed_product(kbuf[:, width:])
 
-    def gram_copy(k):
+    low, high = pl.ds(0, panel // 2), pl.ds(panel // 2, panel // 2)
+
+    def right_copy(k):
         peer = wrap(me + k, n_rows)
         return pltpu.make_async_remote_copy(
-            src_ref=gram.at[rows_of(peer, TILE), :], dst_ref=gbuf.at[k - 1],
+            src_ref=gram.at[rows_of(peer, TILE), high], dst_ref=gbuf.at[me],
             send_sem=gsend.at[k], recv_sem=rsem.at[0],
             device_id=(peer, group), device_id_type=MESH,
+        )
+
+    def left_copy(k):
+        to_chip = wrap(chip + k, n_chips)
+        return pltpu.make_async_remote_copy(
+            src_ref=gram.at[rows_of(to_chip, TILE), low], dst_ref=lbuf.at[me],
+            send_sem=lsend.at[k], recv_sem=rsem.at[3],
+            device_id=(to_chip * 2, group), device_id_type=MESH,
         )
 
     def cross_copy(k):
@@ -233,45 +243,98 @@
             device_id=(peer, group), device_id_type=MESH,
         )
 
-    def whole_copy(k):
-        return pltpu.make_async_remote_copy(
-            src_ref=total_gram.at[rows_of(me, TILE), :],
-            dst_ref=total_gram.at[rows_of(me, TILE), :],
-            send_sem=wsend.at[k], recv_sem=rsem.at[2],
+    def right_whole(k):
+        mine = total_gram.at[rows_of(me, TILE), high]
+        return pltpu.make_async_remote_copy(
+            src_ref=mine, dst_ref=mine, send_sem=wsend.at[k], recv_sem=rsem.at[2],
             device_id=(wrap(me + k, n_rows), group), device_id_type=MESH,
         )
 
-    each(1, n_rows, lambda k: gram_copy(k).start())
+    def left_whole(k):
+        mine = total_gram.at[rows_of(chip, TILE), low]
+        return pltpu.make_async_remote_copy(
+            src_ref=mine, dst_ref=mine, send_sem=vsend.at[k], recv_sem=rsem.at[4],
+            device_id=(wrap(me + k, n_rows), group), device_id_type=MESH,
+        )
+
+    def landed(ref, sem):
+        pltpu.make_async_copy(ref, ref, sem).wait()
+
+    each(1, n_rows, lambda k: right_copy(k).start())
+    each(1, n_chips, lambda k: left_copy(k).start())
+
+    @pl.when(core == 1)
+    def _():
+        left_copy(0).start()
+
+    total_gram[panel // 2 :, : panel // 2] = jnp.zeros((panel // 2, panel // 2), F32)
+    gbuf[me] = gram[rows_of(me, TILE), panel // 2 :]
+    lbuf[me] = gram[rows_of(chip, TILE), : panel // 2]
     product = transposed_product(kbuf[:, :width])
     for r in range(panel // TILE):
         part = product[r * TILE : (r + 1) * TILE, :]
         cross[r] = jnp.concatenate([part[:, :short], part[:, short:]], axis=0).astype(BF16)
     each(1, n_rows, lambda k: cross_copy(k).start())
-    pltpu.make_async_copy(gbuf, gbuf, rsem.at[0]).wait()
-    total = gram[rows_of(me, TILE), :]
-    for r in range(n_rows - 1):
-        total = total + gbuf[r]
-    total_gram[rows_of(me, TILE), :] = total
-    each(1, n_rows, lambda k: whole_copy(k).start())
+
+    def summed(pieces):
+        total = pieces[0]
+        for r in range(1, n_rows):
+            total = total + pieces[r]
+        return total
+
+    others = pl.ds(0, n_rows - 1)
+    landed(gbuf.at[others], rsem.at[0])
+    total_gram[rows_of(me, TILE), panel // 2 :] = summed(gbuf)
+    each(1, n_rows, lambda k: right_whole(k).start())
+
+    @pl.when(core == 0)
+    def _():
+        landed(lbuf.at[others], rsem.at[3])
+        total_gram[rows_of(chip, TILE), : panel // 2] = summed(lbuf)
+        each(1, n_rows, lambda k: left_whole(k).start())
+
     pltpu.make_async_copy(cbuf, cbuf, rsem.at[1]).wait()
     total = cross[me].astype(F32)
     for r in range(n_rows - 1):
         total = total + cbuf[r].astype(F32)
-    sum_ref[:, :short] = total[:TILE]
-    sum_ref[:, short:] = total[TILE:]
-    arrived = total_gram.at[pl.ds(0, panel - TILE), :]
-    pltpu.make_async_copy(arrived, arrived, rsem.at[2]).wait()
-    whole_ref[...] = total_gram[...]
-
-    def all_sent(k):
-        gram_copy(k).wait_send()
+    sumbuf[:, :short] = total[:TILE]
+    sumbuf[:, short:] = total[TILE:]
+    save_sum = pltpu.make_async_copy(sumbuf, sum_ref, isem.at[3])
+    save_sum.start()
+
+    def early_sent(k):
+        right_copy(k).wait_send()
         cross_copy(k).wait_send()
-        whole_copy(k).wait_send()
-
-    each(1, n_rows, all_sent)
+
+    each(1, n_rows, early_sent)
+    each(1, n_chips, lambda k: left_copy(k).wait_send())
     each(1, n_chips, lambda k: plane_copy(k).wait_send())
     each(0, n_chips, lambda k: core_copy(k).wait_send())
     each(0, blocks, lambda i: save(i).wait())
+    landed(total_gram.at[pl.ds(0, panel - TILE), high], rsem.at[2])
+
+    @pl.when(core == 0)
+    def _():
+        landed(total_gram.at[pl.ds(0, (n_chips - 1) * TILE), low], rsem.at[4])
+
+    @pl.when(core == 1)
+    def _():
+        landed(total_gram.at[pl.ds(0, n_chips * TILE), low], rsem.at[4])
+
+    save_whole = pltpu.make_async_copy(total_gram, whole_ref, isem.at[4])
+    save_whole.start()
+
+    @pl.when(core == 1)
+    def _():
+        left_copy(0).wait_send()
+
+    @pl.when(core == 0)
+    def _():
+        each(1, n_rows, lambda k: left_whole(k).wait_send())
+
+    each(1, n_rows, lambda k: right_whole(k).wait_send())
+    save_sum.wait()
+    save_whole.wait()
 
 
 def gram_pass(panel_pick, env_count, struct_atoms, sparse_desc, descriptors, n_rows, n_cols, block):
@@ -290,7 +353,7 @@
             jax.ShapeDtypeStruct((TILE, width), F32),
         ),
         in_specs=[hbm, hbm, vmem, hbm, hbm],
-        out_specs=(hbm, vmem, vmem),
+        out_specs=(hbm, hbm, hbm),
         scratch_shapes=[
             pltpu.VMEM((slots, depth), BF16),
             pltpu.VMEM((slots, width + panel), BF16),
@@ -301,15 +364,17 @@
             pltpu.VMEM((panel, depth), BF16),
             pltpu.VMEM((n_cols, 16, depth // 2), BF16),
             pltpu.VMEM((panel, panel), F32),
-            pltpu.VMEM((n_rows - 1, TILE, panel), F32),
+            pltpu.VMEM((n_rows, TILE, panel // 2), F32),
+            pltpu.VMEM((n_rows, TILE, panel // 2), F32),
             pltpu.VMEM((panel, panel), F32),
             pltpu.VMEM((n_rows, 2 * TILE, short), BF16),
             pltpu.VMEM((n_rows - 1, 2 * TILE, short), BF16),
+            pltpu.VMEM((TILE, width), F32),
             pltpu.SMEM((panel,), jnp.int32),
             pltpu.SMEM((1,), jnp.int32),
             dma((slots // block,)),
             dma((slots // block,)),
-            dma((3,)),
+            dma((5,)),
             dma((n_cols - 1,)),
             dma((n_cols - 1,)),
             dma((n_chips,)),
@@ -318,7 +383,9 @@
             dma((n_rows,)),
             dma((n_rows,)),
             dma((n_rows,)),
-            dma((3,)),
+            dma((n_chips,)),
+            dma((n_rows,)),
+            dma((5,)),
         ],
         compiler_params=pltpu.CompilerParams(
             collective_id=0, has_side_effects=True, vmem_limit_bytes=56 * MIB

time: 52.2 us -> 50.9 us (0.975)
  Pallas kernels: 50.5 us -> 49.3 us
    pallas_call x1, Pallas kernels: 41 us -> 39.8 us  [gram_pass(): pl.pallas_call(functools.partial(gram_kernel, n_rows, n_cols, slots // 3...]
where the time goes in v2:
time: 50.9 us; the launch traced here: 50.7 us
  Pallas kernels  49.3 us (97%)
  between operations  1.45 us (3%)
    pallas_call x1, Pallas kernels, gram_pass(): pl.pallas_call(functools.partial(gram_kernel, n_rows, n_cols, slots // 3...  39.8 us
    pallas_call x1, Pallas kernels, factor_pass(): pl.pallas_call(factor_kernel, out_shape=(jax.ShapeDtypeStruct((TILE, size...  9.55 us

profile of v2, /device:TPU:1, one launch (start us, length us, event | category | flops | bytes accessed | tf_op | source)
XLA Modules:
  0.0 50.7 jit_solution(10563389587473545590)
XLA Ops:
  1.3 39.8 %gram_pass.1 = (bf16[6144,512]{1,0:T(8,128)(2,1)}, f32[256,256]{1,0:T(8,128)}, f32[8,512]{1,0:T(8,128)}) custom-call(s32[256]{0:T(256)} %pick_ref.1, s32[1]{0:T(128)S(6)} %copy.8.count_ref, s32[48,128]{1,0:T(8,128)} %bitcast.1, bf16[512,1024]{1,0:T(8,128)(2,1)} %sparse_ref.1, bf16[6144,1024]{1,0:T(8,128)(2,1)} %x_ref.1), custom_call_target="tpu_custom_call" | custom-call | tf_op jit(solution)/shard_map/gram_pass/pallas_call | solution.py:348
  41.0 9.5 %factor_pass.1 = (f32[8,256]{1,0:T(8,128)}, bf16[6144,512]{1,0:T(8,128)(2,1)}, f32[8,512]{1,0:T(8,128)}) custom-call(f32[256,256]{1,0:T(8,128)} %get-tuple-element.9.gram_ref, bf16[6144,512]{1,0:T(8,128)(2,1)} %get-tuple-element.10.rows_ref, f32[8,512]{1,0:T(8,128)} %get-tuple-element.11.sum_ref), custom_call_target="tpu_custom_call" | custom-call | tf_op jit(solution)/shard_map/factor_pass/pallas_call | solution.py:536

commit v3 on v2

--- a/solution.py
+++ b/solution.py
@@ -37,7 +37,7 @@
     n_rows, n_cols, env_total, block,
     pick_ref, count_ref, atoms_ref, sparse_ref, x_ref,
     rows_ref, whole_ref, sum_ref,
-    xbuf, kbuf, partial, factor, columns, units, gathered, zbuf, gram, gbuf, lbuf, total_gram, cross, cbuf, sumbuf,
+    xbuf, kbuf, partial, factor, columns, units, gathered, zbuf, gram, gbuf, lbuf, total_gram, cross, paired, both, cbuf, sumbuf,
     picks, count, xsem, osem, isem, zsend, zrecv, psend, fsend, precv, gsend, csend, wsend, lsend, vsend, rsem,
 ):
     me = lax.axis_index("rows")
@@ -61,8 +61,6 @@
         at = rows_of(i, block)
         return pltpu.make_async_copy(x_ref.at[at, :], xbuf.at[at, :], xsem.at[i])
 
-    each(0, slots // block, lambda i: load(i).start())
-
     barrier = pltpu.get_barrier_semaphore()
     each(1, n_rows, lambda k: pl.semaphore_signal(
         barrier, inc=1, device_id=(wrap(me + k, n_rows), group), device_id_type=MESH))
@@ -72,8 +70,9 @@
         )
 
     load_units.wait()
-
     load_picks.wait()
+    each(0, slots // block, lambda i: load(i).start())
+
     column = lax.broadcasted_iota(jnp.int32, (16, width), 1) + group * width
     row = lax.broadcasted_iota(jnp.int32, (16, width), 0)
     wanted = jnp.zeros((16, width), jnp.int32)
@@ -235,12 +234,19 @@
             device_id=(to_chip * 2, group), device_id_type=MESH,
         )
 
+    def pair_copy():
+        return pltpu.make_async_remote_copy(
+            src_ref=cross.at[1 - core], dst_ref=paired,
+            send_sem=csend.at[0], recv_sem=rsem.at[5],
+            device_id=(chip * 2 + 1 - core, group), device_id_type=MESH,
+        )
+
     def cross_copy(k):
-        peer = wrap(me + k, n_rows)
-        return pltpu.make_async_remote_copy(
-            src_ref=cross.at[peer], dst_ref=cbuf.at[k - 1],
+        to_chip = wrap(chip + k, n_chips)
+        return pltpu.make_async_remote_copy(
+            src_ref=both.at[to_chip], dst_ref=cbuf.at[k - 1],
             send_sem=csend.at[k], recv_sem=rsem.at[1],
-            device_id=(peer, group), device_id_type=MESH,
+            device_id=(to_chip * 2 + core, group), device_id_type=MESH,
         )
 
     def right_whole(k):
@@ -273,8 +279,11 @@
     product = transposed_product(kbuf[:, :width])
     for r in range(panel // TILE):
         part = product[r * TILE : (r + 1) * TILE, :]
-        cross[r] = jnp.concatenate([part[:, :short], part[:, short:]], axis=0).astype(BF16)
-    each(1, n_rows, lambda k: cross_copy(k).start())
+        cross[r % 2, r // 2] = jnp.concatenate([part[:, :short], part[:, short:]], axis=0).astype(BF16)
+    pair_copy().start()
+    pair_copy().wait()
+    both[...] = (cross[core].astype(F32) + paired[...].astype(F32)).astype(BF16)
+    each(1, n_chips, lambda k: cross_copy(k).start())
 
     def summed(pieces):
         total = pieces[0]
@@ -294,19 +303,16 @@
         each(1, n_rows, lambda k: left_whole(k).start())
 
     pltpu.make_async_copy(cbuf, cbuf, rsem.at[1]).wait()
-    total = cross[me].astype(F32)
-    for r in range(n_rows - 1):
+    total = both[chip].astype(F32)
+    for r in range(n_chips - 1):
         total = total + cbuf[r].astype(F32)
     sumbuf[:, :short] = total[:TILE]
     sumbuf[:, short:] = total[TILE:]
     save_sum = pltpu.make_async_copy(sumbuf, sum_ref, isem.at[3])
     save_sum.start()
 
-    def early_sent(k):
-        right_copy(k).wait_send()
-        cross_copy(k).wait_send()
-
-    each(1, n_rows, early_sent)
+    each(1, n_rows, lambda k: right_copy(k).wait_send())
+    each(1, n_chips, lambda k: cross_copy(k).wait_send())
     each(1, n_chips, lambda k: left_copy(k).wait_send())
     each(1, n_chips, lambda k: plane_copy(k).wait_send())
     each(0, n_chips, lambda k: core_copy(k).wait_send())
@@ -367,8 +373,10 @@
             pltpu.VMEM((n_rows, TILE, panel // 2), F32),
             pltpu.VMEM((n_rows, TILE, panel // 2), F32),
             pltpu.VMEM((panel, panel), F32),
-            pltpu.VMEM((n_rows, 2 * TILE, short), BF16),
-            pltpu.VMEM((n_rows - 1, 2 * TILE, short), BF16),
+            pltpu.VMEM((2, n_chips, 2 * TILE, short), BF16),
+            pltpu.VMEM((n_chips, 2 * TILE, short), BF16),
+            pltpu.VMEM((n_chips, 2 * TILE, short), BF16),
+            pltpu.VMEM((n_chips - 1, 2 * TILE, short), BF16),
             pltpu.VMEM((TILE, width), F32),
             pltpu.SMEM((panel,), jnp.int32),
             pltpu.SMEM((1,), jnp.int32),
@@ -385,7 +393,7 @@
             dma((n_rows,)),
             dma((n_chips,)),
             dma((n_rows,)),
-            dma((5,)),
+            dma((6,)),
         ],
         compiler_params=pltpu.CompilerParams(
             collective_id=0, has_side_effects=True, vmem_limit_bytes=56 * MIB

time: 50.9 us -> 50.8 us (level)
  no operation moved by 1% of the time
where the time goes in v3:
time: 50.8 us; the launch traced here: 50.6 us
  Pallas kernels  49.2 us (97%)
  between operations  1.45 us (3%)
    pallas_call x1, Pallas kernels, gram_pass(): pl.pallas_call(functools.partial(gram_kernel, n_rows, n_cols, slots // 3...  39.6 us
    pallas_call x1, Pallas kernels, factor_pass(): pl.pallas_call(factor_kernel, out_shape=(jax.ShapeDtypeStruct((TILE, size...  9.55 us

profile of v3, /device:TPU:1, one launch (start us, length us, event | category | flops | bytes accessed | tf_op | source)
XLA Modules:
  0.0 50.6 jit_solution(17239637820622452362)
XLA Ops:
  1.3 39.6 %gram_pass.1 = (bf16[6144,512]{1,0:T(8,128)(2,1)}, f32[256,256]{1,0:T(8,128)}, f32[8,512]{1,0:T(8,128)}) custom-call(s32[256]{0:T(256)} %pick_ref.1, s32[1]{0:T(128)S(6)} %copy.8.count_ref, s32[48,128]{1,0:T(8,128)} %bitcast.1, bf16[512,1024]{1,0:T(8,128)(2,1)} %sparse_ref.1, bf16[6144,1024]{1,0:T(8,128)(2,1)} %x_ref.1), custom_call_target="tpu_custom_call" | custom-call | tf_op jit(solution)/shard_map/gram_pass/pallas_call | solution.py:354
  40.9 9.5 %factor_pass.1 = (f32[8,256]{1,0:T(8,128)}, bf16[6144,512]{1,0:T(8,128)(2,1)}, f32[8,512]{1,0:T(8,128)}) custom-call(f32[256,256]{1,0:T(8,128)} %get-tuple-element.9.gram_ref, bf16[6144,512]{1,0:T(8,128)(2,1)} %get-tuple-element.10.rows_ref, f32[8,512]{1,0:T(8,128)} %get-tuple-element.11.sum_ref), custom_call_target="tpu_custom_call" | custom-call | tf_op jit(solution)/shard_map/factor_pass/pallas_call | solution.py:544
